TPU v7x, 256 devices: a whole 4x4x8 slice. The times are simulated.
256 devices in a mesh: mrow: 32 (over x_hi, z, core), mcol: 8 (over y, x_lo).
Axes of the slice: x: 4 (x_hi: 2, x_lo: 2; x = x_hi * 2 + x_lo), y: 4, z: 8, core: 2. Of those that a mesh axis runs over, the one named last changes fastest.
Arguments:
- queries: bfloat16 [4096, 4096], P('mrow', 'mcol'), may hold values from -6 to 6
- grad_out: bfloat16 [4096, 4096], P('mrow', 'mcol'), may hold values from -6 to 6
- attn_out: bfloat16 [4096, 4096], P('mrow', 'mcol'), may hold values from -2 to 2
- log_sum: float32 [4096, 32], P('mrow', 'mcol'), as said below
- memory_keys: bfloat16 [256, 128, 1024], P('mrow', 'mcol'), may hold values from -6 to 6
- memory_values: bfloat16 [256, 128, 1024], P('mrow', 'mcol'), may hold values from -6 to 6
Outputs:
- grad_queries: float32 [4096, 4096], P('mrow', 'mcol')
Inputs may be any that keep to these rules, and one draw needn't show every extreme that they name: `log_sum`: each entry is the natural logarithm of 32768, plus 0 to 1.
All inputs are finite; a program needn't handle non-finite values.
Results may differ from a plain program's by a relative error of at most 0.0023.
Values may be sent and summed in bfloat16 or wider, within the bound.
A program may use at most 64 MiB of HBM per device.

v0:
```python
import jax
import jax.numpy as jnp
from jax import lax
from jax.sharding import PartitionSpec as P

H = 32
KVH = 8
HD = 128


def divisor_at_most(total, limit):
    best = 1
    for size in range(1, total + 1):
        if total % size == 0 and size <= limit:
            best = size
    return best


def head_terms(query_heads, grad_heads, log_heads, dot_heads, mem_keys, mem_values):
    scaling = HD ** (-0.5)
    scores = (
        jnp.einsum("tkgd,ekd->kgte", query_heads, mem_keys, preferred_element_type=jnp.float32)
        * scaling
    )
    weights = jnp.exp(scores - log_heads[..., None])
    grad_probs = jnp.einsum(
        "tkgd,ekd->kgte", grad_heads, mem_values, preferred_element_type=jnp.float32
    )
    grad_scores = (weights * (grad_probs - dot_heads[..., None])).astype(jnp.bfloat16)
    return scaling * jnp.einsum(
        "kgte,ekd->tkgd", grad_scores, mem_keys, preferred_element_type=jnp.float32
    )


def block_terms(stacked, log_rows, dot_rows, mem_keys, mem_values):
    row_count = stacked.shape[0]
    heads_here = log_rows.shape[1]
    per_group = H // KVH
    kv_here = heads_here // per_group
    entries = mem_keys.shape[0]
    step = divisor_at_most(row_count, max(1, 2**21 // (heads_here * entries)))
    count = row_count // step
    query_heads = stacked[:, 0].reshape(count, step, kv_here, per_group, HD)
    grad_heads = stacked[:, 1].reshape(count, step, kv_here, per_group, HD)
    log_heads = log_rows.reshape(count, step, kv_here, per_group).transpose(0, 2, 3, 1)
    dot_heads = dot_rows.reshape(count, step, kv_here, per_group).transpose(0, 2, 3, 1)

    def one_block(inputs):
        query_part, grad_part, log_part, dot_part = inputs
        return head_terms(query_part, grad_part, log_part, dot_part, mem_keys, mem_values)

    terms = lax.map(one_block, (query_heads, grad_heads, log_heads, dot_heads))
    return terms.reshape(row_count, heads_here * HD)


def body(queries, grad_out, attn_out, log_sum, memory_keys, memory_values):
    token_count = queries.shape[0]
    heads_here = log_sum.shape[1]
    kv_here = heads_here // (H // KVH)
    out_dot = jnp.sum(
        (grad_out.astype(jnp.float32) * attn_out.astype(jnp.float32)).reshape(
            token_count, heads_here, HD
        ),
        axis=-1,
    )
    key_tiles = memory_keys.reshape(memory_keys.shape[0], memory_keys.shape[1], KVH, HD)
    value_tiles = memory_values.reshape(memory_values.shape[0], memory_values.shape[1], KVH, HD)
    own_keys, own_values = (
        lax.all_to_all(key_tiles, "mcol", split_axis=2, concat_axis=1, tiled=True),
        lax.all_to_all(value_tiles, "mcol", split_axis=2, concat_axis=1, tiled=True),
    )
    mem_keys = own_keys.reshape(-1, kv_here, HD)
    mem_values = own_values.reshape(-1, kv_here, HD)
    stacked = jnp.stack([queries, grad_out], axis=1)
    gathered_stats = (
        lax.all_gather(log_sum, "mrow", axis=0, tiled=True),
        lax.all_gather(out_dot, "mrow", axis=0, tiled=True),
    )
    log_rows = gathered_stats[0]
    dot_rows = gathered_stats[1]
    partial_grad = block_terms(
        lax.all_gather(stacked, "mrow", axis=0, tiled=True),
        log_rows,
        dot_rows,
        mem_keys,
        mem_values,
    )
    result = lax.psum_scatter(partial_grad, "mrow", scatter_dimension=0, tiled=True)
    return result


def solution(mesh):
    return jax.shard_map(
        body,
        mesh=mesh,
        in_specs=(
            P("mrow", "mcol"),
            P("mrow", "mcol"),
            P("mrow", "mcol"),
            P("mrow", "mcol"),
            P("mrow", "mcol", None),
            P("mrow", "mcol", None),
        ),
        out_specs=P("mrow", "mcol"),
        check_vma=False,
    )
```

profile of v0, /device:TPU:8, one launch (start us, length us, event | category | flops | bytes accessed | tf_op | source)
XLA Modules:
  0.0 411.1 jit_solution(14667618074723072190)
XLA Ops:
  9.1 5.8 %all-to-all-start = ((bf16[8,16,8,128]{3,1,0,2:T(8,128)(2,1)}), bf16[8,16,8,128]{3,1,0,2:T(8,128)(2,1)S(1)}, u32[]{:S(2)}, u32[]{:S(2)}) async-start(bf16[8,16,8,128]{3,1,0,2:T(8,128)(2,1)} %copy_bitcast_fusion.8), calls=%async_computation | async-start | bytes 524288 | tf_op jit(solution)/shard_map/all_to_all | solution.py:69
  20.7 4.8 %all-to-all-start.1 = ((bf16[8,16,8,128]{3,1,0,2:T(8,128)(2,1)}), bf16[8,16,8,128]{3,1,0,2:T(8,128)(2,1)S(1)}, u32[]{:S(2)}, u32[]{:S(2)}) async-start(bf16[8,16,8,128]{3,1,0,2:T(8,128)(2,1)} %copy_bitcast_fusion.7), calls=%async_computation.1 | async-start | bytes 524288 | tf_op jit(solution)/shard_map/all_to_all | solution.py:70
  26.8 52.1 %all_gather.11 = f32[4096,4]{1,0:T(8,128)S(1)} all-gather(f32[128,4]{1,0:T(8,128)S(1)} %reduce_sum.9), channel_id=1, replica_groups=mesh['mrow'=32,'mcol'=8] {'mrow'}, dimensions={0}, use_global_device_ids=true | all-gather | bytes 67584 | tf_op jit(solution)/shard_map/all_gather | solution.py:77
  79.6 37.0 %all_gather.10 = f32[4096,4]{0,1:T(4,128)S(1)} all-gather(f32[128,4]{0,1:T(4,128)S(1)} %copy-done.1), channel_id=1, replica_groups=mesh['mrow'=32,'mcol'=8] {'mrow'}, dimensions={0}, use_global_device_ids=true | all-gather | bytes 67584 | tf_op jit(solution)/shard_map/all_gather | solution.py:76
  117.0 5.7 %fusion.20 = (bf16[4096,1,512]{2,0,1:T(8,128)(2,1)}, bf16[4096,1,512]{2,0,1:T(8,128)(2,1)}) fusion(bf16[4096,2,512]{2,0,1:T(8,128)(2,1)} %all-gather.2.cloned.1.call-done), kind=kLoop, calls=%fused_computation.28 | loop fusion | bytes 16777216 | tf_op jit(solution)/shard_map/slice | solution.py:44
  122.8 6.9 %reshape.69 = bf16[8,512,1,4,128]{4,3,1,0,2:T(4,128)(2,1)} reshape(bf16[4096,1,512]{2,0,1:T(8,128)(2,1)} %get-tuple-element.93) | data formatting | bytes 8388608 | tf_op jit(solution)/shard_map/reshape;squeeze | solution.py:43
  129.7 6.9 %reshape.70 = bf16[8,512,1,4,128]{4,3,1,0,2:T(4,128)(2,1)} reshape(bf16[4096,1,512]{2,0,1:T(8,128)(2,1)} %get-tuple-element.92) | data formatting | bytes 8388608 | tf_op jit(solution)/shard_map/reshape;squeeze | solution.py:44
  136.6 108.8 %while.10 = (s32[]{:T(128)}, f32[8,512,1,4,128]{4,3,1,0,2:T(4,128)}, bf16[8,512,1,4,128]{4,3,1,0,2:T(4,128)(2,1)}, bf16[1024,1,128]{2,0,1:T(8,128)(2,1)S(1)}, f3...) while((s32[]{:T(128)}, ...), condition=%wide.region_2.3_spmd, body=%wide.region_1.2_spmd.sunk | while | flops 1621360640 | bytes 23921256 | solution.py:52
  138.2 4.5 %fusion.33 = f32[512,4,1024]{2,0,1:T(8,128)} fusion(bf16[1,512,1,4,128]{4,3,1,0,2:T(4,128)(2,1)S(1)} %get-tuple-element.147, bf16[1024,1,128]{2,0,1:T(8,128)(2,1)S(1)} %get-tuple-element.172), kind=kOutput, calls=%fused_computation.13.clone.1 | convolution fusion | flops 536870912 | bytes 9175040 | tf_op jit(solution)/shard_map/while/body/eval_jaxpr/tkgd,ekd->kgte/dot_general | solution.py:22
  142.7 5.8 %fusion.34 = f32[1,512,1,4,128]{4,1,3,2,0:T(8,128)S(1)} fusion(f32[512,4,1024]{2,0,1:T(8,128)} %fusion.33, f32[4,512]{1,0:T(4,128)S(1)} %get-tuple-element.148, f32[4,512]{1,0:T(4,128)S(1)} %get-tuple-element.149, bf16[1,512,1,4,128]{4,3,1,0,2:T(4,128)(2,1)S(1)} %get-tuple-element.150, bf16[1024,1,128]{2,0,1:T(8,128)(2,1)S(1)} %get-tuple-element.175, ...), kind=kOutput, calls=%fused_computation.9.clone.1 | convolution fusion | flops 1084489728 | bytes 10502144 | tf_op jit(solution)/shard_map/while/body/eval_jaxpr/kgte,ekd->tkgd/dot_general | solution.py:30
  151.8 4.5 %fusion.33 = f32[512,4,1024]{2,0,1:T(8,128)} fusion(bf16[1,512,1,4,128]{4,3,1,0,2:T(4,128)(2,1)S(1)} %get-tuple-element.147, bf16[1024,1,128]{2,0,1:T(8,128)(2,1)S(1)} %get-tuple-element.172), kind=kOutput, calls=%fused_computation.13.clone.1 | convolution fusion | flops 536870912 | bytes 9175040 | tf_op jit(solution)/shard_map/while/body/eval_jaxpr/tkgd,ekd->kgte/dot_general | solution.py:22
  156.2 5.8 %fusion.34 = f32[1,512,1,4,128]{4,1,3,2,0:T(8,128)S(1)} fusion(f32[512,4,1024]{2,0,1:T(8,128)} %fusion.33, f32[4,512]{1,0:T(4,128)S(1)} %get-tuple-element.148, f32[4,512]{1,0:T(4,128)S(1)} %get-tuple-element.149, bf16[1,512,1,4,128]{4,3,1,0,2:T(4,128)(2,1)S(1)} %get-tuple-element.150, bf16[1024,1,128]{2,0,1:T(8,128)(2,1)S(1)} %get-tuple-element.175, ...), kind=kOutput, calls=%fused_computation.9.clone.1 | convolution fusion | flops 1084489728 | bytes 10502144 | tf_op jit(solution)/shard_map/while/body/eval_jaxpr/kgte,ekd->tkgd/dot_general | solution.py:30
  165.4 4.5 %fusion.33 = f32[512,4,1024]{2,0,1:T(8,128)} fusion(bf16[1,512,1,4,128]{4,3,1,0,2:T(4,128)(2,1)S(1)} %get-tuple-element.147, bf16[1024,1,128]{2,0,1:T(8,128)(2,1)S(1)} %get-tuple-element.172), kind=kOutput, calls=%fused_computation.13.clone.1 | convolution fusion | flops 536870912 | bytes 9175040 | tf_op jit(solution)/shard_map/while/body/eval_jaxpr/tkgd,ekd->kgte/dot_general | solution.py:22
  169.9 5.8 %fusion.34 = f32[1,512,1,4,128]{4,1,3,2,0:T(8,128)S(1)} fusion(f32[512,4,1024]{2,0,1:T(8,128)} %fusion.33, f32[4,512]{1,0:T(4,128)S(1)} %get-tuple-element.148, f32[4,512]{1,0:T(4,128)S(1)} %get-tuple-element.149, bf16[1,512,1,4,128]{4,3,1,0,2:T(4,128)(2,1)S(1)} %get-tuple-element.150, bf16[1024,1,128]{2,0,1:T(8,128)(2,1)S(1)} %get-tuple-element.175, ...), kind=kOutput, calls=%fused_computation.9.clone.1 | convolution fusion | flops 1084489728 | bytes 10502144 | tf_op jit(solution)/shard_map/while/body/eval_jaxpr/kgte,ekd->tkgd/dot_general | solution.py:30
  183.5 5.8 %fusion.34 = f32[1,512,1,4,128]{4,1,3,2,0:T(8,128)S(1)} fusion(f32[512,4,1024]{2,0,1:T(8,128)} %fusion.33, f32[4,512]{1,0:T(4,128)S(1)} %get-tuple-element.148, f32[4,512]{1,0:T(4,128)S(1)} %get-tuple-element.149, bf16[1,512,1,4,128]{4,3,1,0,2:T(4,128)(2,1)S(1)} %get-tuple-element.150, bf16[1024,1,128]{2,0,1:T(8,128)(2,1)S(1)} %get-tuple-element.175, ...), kind=kOutput, calls=%fused_computation.9.clone.1 | convolution fusion | flops 1084489728 | bytes 10502144 | tf_op jit(solution)/shard_map/while/body/eval_jaxpr/kgte,ekd->tkgd/dot_general | solution.py:30
  192.6 4.5 %fusion.33 = f32[512,4,1024]{2,0,1:T(8,128)} fusion(bf16[1,512,1,4,128]{4,3,1,0,2:T(4,128)(2,1)S(1)} %get-tuple-element.147, bf16[1024,1,128]{2,0,1:T(8,128)(2,1)S(1)} %get-tuple-element.172), kind=kOutput, calls=%fused_computation.13.clone.1 | convolution fusion | flops 536870912 | bytes 9175040 | tf_op jit(solution)/shard_map/while/body/eval_jaxpr/tkgd,ekd->kgte/dot_general | solution.py:22
  197.1 5.8 %fusion.34 = f32[1,512,1,4,128]{4,1,3,2,0:T(8,128)S(1)} fusion(f32[512,4,1024]{2,0,1:T(8,128)} %fusion.33, f32[4,512]{1,0:T(4,128)S(1)} %get-tuple-element.148, f32[4,512]{1,0:T(4,128)S(1)} %get-tuple-element.149, bf16[1,512,1,4,128]{4,3,1,0,2:T(4,128)(2,1)S(1)} %get-tuple-element.150, bf16[1024,1,128]{2,0,1:T(8,128)(2,1)S(1)} %get-tuple-element.175, ...), kind=kOutput, calls=%fused_computation.9.clone.1 | convolution fusion | flops 1084489728 | bytes 10502144 | tf_op jit(solution)/shard_map/while/body/eval_jaxpr/kgte,ekd->tkgd/dot_general | solution.py:30
  206.1 4.5 %fusion.33 = f32[512,4,1024]{2,0,1:T(8,128)} fusion(bf16[1,512,1,4,128]{4,3,1,0,2:T(4,128)(2,1)S(1)} %get-tuple-element.147, bf16[1024,1,128]{2,0,1:T(8,128)(2,1)S(1)} %get-tuple-element.172), kind=kOutput, calls=%fused_computation.13.clone.1 | convolution fusion | flops 536870912 | bytes 9175040 | tf_op jit(solution)/shard_map/while/body/eval_jaxpr/tkgd,ekd->kgte/dot_general | solution.py:22
  210.6 5.8 %fusion.34 = f32[1,512,1,4,128]{4,1,3,2,0:T(8,128)S(1)} fusion(f32[512,4,1024]{2,0,1:T(8,128)} %fusion.33, f32[4,512]{1,0:T(4,128)S(1)} %get-tuple-element.148, f32[4,512]{1,0:T(4,128)S(1)} %get-tuple-element.149, bf16[1,512,1,4,128]{4,3,1,0,2:T(4,128)(2,1)S(1)} %get-tuple-element.150, bf16[1024,1,128]{2,0,1:T(8,128)(2,1)S(1)} %get-tuple-element.175, ...), kind=kOutput, calls=%fused_computation.9.clone.1 | convolution fusion | flops 1084489728 | bytes 10502144 | tf_op jit(solution)/shard_map/while/body/eval_jaxpr/kgte,ekd->tkgd/dot_general | solution.py:30
  219.8 4.5 %fusion.33 = f32[512,4,1024]{2,0,1:T(8,128)} fusion(bf16[1,512,1,4,128]{4,3,1,0,2:T(4,128)(2,1)S(1)} %get-tuple-element.147, bf16[1024,1,128]{2,0,1:T(8,128)(2,1)S(1)} %get-tuple-element.172), kind=kOutput, calls=%fused_computation.13.clone.1 | convolution fusion | flops 536870912 | bytes 9175040 | tf_op jit(solution)/shard_map/while/body/eval_jaxpr/tkgd,ekd->kgte/dot_general | solution.py:22
  224.2 5.8 %fusion.34 = f32[1,512,1,4,128]{4,1,3,2,0:T(8,128)S(1)} fusion(f32[512,4,1024]{2,0,1:T(8,128)} %fusion.33, f32[4,512]{1,0:T(4,128)S(1)} %get-tuple-element.148, f32[4,512]{1,0:T(4,128)S(1)} %get-tuple-element.149, bf16[1,512,1,4,128]{4,3,1,0,2:T(4,128)(2,1)S(1)} %get-tuple-element.150, bf16[1024,1,128]{2,0,1:T(8,128)(2,1)S(1)} %get-tuple-element.175, ...), kind=kOutput, calls=%fused_computation.9.clone.1 | convolution fusion | flops 1084489728 | bytes 10502144 | tf_op jit(solution)/shard_map/while/body/eval_jaxpr/kgte,ekd->tkgd/dot_general | solution.py:30
  237.8 5.8 %fusion.34 = f32[1,512,1,4,128]{4,1,3,2,0:T(8,128)S(1)} fusion(f32[512,4,1024]{2,0,1:T(8,128)} %fusion.33, f32[4,512]{1,0:T(4,128)S(1)} %get-tuple-element.148, f32[4,512]{1,0:T(4,128)S(1)} %get-tuple-element.149, bf16[1,512,1,4,128]{4,3,1,0,2:T(4,128)(2,1)S(1)} %get-tuple-element.150, bf16[1024,1,128]{2,0,1:T(8,128)(2,1)S(1)} %get-tuple-element.175, ...), kind=kOutput, calls=%fused_computation.9.clone.1 | convolution fusion | flops 1084489728 | bytes 10502144 | tf_op jit(solution)/shard_map/while/body/eval_jaxpr/kgte,ekd->tkgd/dot_general | solution.py:30
  245.4 7.6 %copy.60 = f32[512,8,4,128]{3,1,2,0:T(8,128)} copy(f32[512,8,4,128]{3,2,1,0:T(4,128)} %bitcast.130) | data formatting | bytes 16777216
  253.0 151.2 %reduce-scatter.2.cloned.1.call-done = f32[128,512]{1,0:T(8,128)} async-done(((f32[4096,512]{1,0:T(8,128)}), f32[128,512]{1,0:T(8,128)}) %reduce-scatter.2.cloned.1.call-update) | async-done | bytes 262160 | tf_op jit(solution)/shard_map/reduce_scatter | solution.py:88
  (55 shorter events, 45.7 us)
Async XLA Ops:
  6.5 1.8 copy-start
  6.5 73.0 %copy-start.1 = (f32[128,4]{0,1:T(4,128)S(1)}, f32[128,4]{0,1:T(4,128)}, u32[]{:S(2)}) copy-start(f32[128,4]{0,1:T(4,128)} %param.11) | copy-start | bytes 6148
  6.5 110.5 %all-gather.2.cloned.1.call-start = ((), (), s32[]{:S(2)}) async-start(), calls=%async_computation.3 | async-start | bytes 8650752 | tf_op jit(solution)/shard_map/all_gather | solution.py:82
  9.1 11.6 %all-to-all-start = ((bf16[8,16,8,128]{3,1,0,2:T(8,128)(2,1)}), bf16[8,16,8,128]{3,1,0,2:T(8,128)(2,1)S(1)}, u32[]{:S(2)}, u32[]{:S(2)}) async-start(bf16[8,16,8,128]{3,1,0,2:T(8,128)(2,1)} %copy_bitcast_fusion.8), calls=%async_computation | async-start | bytes 524288 | tf_op jit(solution)/shard_map/all_to_all | solution.py:69
  20.7 95.9 %all-to-all-start.1 = ((bf16[8,16,8,128]{3,1,0,2:T(8,128)(2,1)}), bf16[8,16,8,128]{3,1,0,2:T(8,128)(2,1)S(1)}, u32[]{:S(2)}, u32[]{:S(2)}) async-start(bf16[8,16,8,128]{3,1,0,2:T(8,128)(2,1)} %copy_bitcast_fusion.7), calls=%async_computation.1 | async-start | bytes 524288 | tf_op jit(solution)/shard_map/all_to_all | solution.py:70
  25.5 378.7 %reduce-scatter.2.cloned.1.call-start = ((), (), s32[]{:S(2)}) async-start(), calls=%async_computation.4 | async-start | bytes 8650752 | tf_op jit(solution)/shard_map/reduce_scatter | solution.py:88
Sparse Core Ops, SparseCore 0:
  10.2 106.8 all-gather.1
  253.1 151.0 reduce-scatter.1
where the time goes:
time: 412 us; the launch traced here: 411 us
  waiting for transfers between devices  156 us (38%)
  blocking collectives  89.1 us (22%)
  matrix products  82.5 us (20%)
  local copies, waits for them, and re-layouts  56.5 us (14%)
  between operations  13.5 us (3%)
  starting transfers between devices  10.7 us (3%)
    reduce_scatter x1, waiting for transfers between devices, body(): lax.psum_scatter(partial_grad, 'mrow', scatter_dimension=0, tiled=True)  151 us
    all_gather x1, blocking collectives, body(): lax.all_gather(out_dot, 'mrow', axis=0, tiled=True)  52.1 us
    dot_general x8, matrix products, head_terms(): jnp.einsum('kgte,ekd->tkgd', grad_scores, mem_keys, preferred_element_typ...  46.7 us
    all_gather x1, blocking collectives, body(): lax.all_gather(log_sum, 'mrow', axis=0, tiled=True)  37 us
    dot_general x8, matrix products, head_terms(): jnp.einsum('tkgd,ekd->kgte', query_heads, mem_keys, preferred_element_typ...  35.8 us
    dynamic_update_slice x8, local copies, waits for them, and re-layouts, block_terms(): terms = lax.map(one_block, (query_heads, grad_heads, log_heads, dot_heads))  13.4 us
    dynamic_slice x16, local copies, waits for them, and re-layouts, block_terms(): terms = lax.map(one_block, (query_heads, grad_heads, log_heads, dot_heads))  12.6 us
  transfers between devices with their start and end apart: 4, of which 3 were waited for; matrix products, arithmetic and copies ran while one was open for 1% of the time, Pallas kernels for 0%

commit v1 on v0

--- a/solution.py
+++ b/solution.py
@@ -6,6 +6,11 @@
 H = 32
 KVH = 8
 HD = 128
+
+
+def swapped_in(array, name, dim):
+    outgoing = jnp.stack([array] * lax.axis_size(name))
+    return jnp.concatenate(lax.all_to_all(outgoing, name, 0, 0), axis=dim)
 
 
 def divisor_at_most(total, limit):
@@ -74,7 +79,7 @@
     stacked = jnp.stack([queries, grad_out], axis=1)
     gathered_stats = (
         lax.all_gather(log_sum, "mrow", axis=0, tiled=True),
-        lax.all_gather(out_dot, "mrow", axis=0, tiled=True),
+        swapped_in(out_dot, "mrow", 0),
     )
     log_rows = gathered_stats[0]
     dot_rows = gathered_stats[1]

time: 412 us -> 409 us (level)
  blocking collectives: 89.1 us -> 38.1 us
  waiting for transfers between devices: 156 us -> 193 us
  starting transfers between devices: 10.7 us -> 21.4 us
    all_gather x1 -> x0, blocking collectives: 52.1 us -> none  [body(): lax.all_gather(out_dot, 'mrow', axis=0, tiled=True)]
    all_gather x1, waiting for transfers between devices: 0.39 us -> 28.6 us  [body(): lax.all_gather(stacked, 'mrow', axis=0, tiled=True)]
    all_to_all x0 -> x1, starting transfers between devices: none -> 11.3 us  [swapped_in(): return jnp.concatenate(lax.all_to_all(outgoing, name, 0, 0), axis=dim)]
    all_to_all x0 -> x1, waiting for transfers between devices: none -> 9.92 us  [swapped_in(): return jnp.concatenate(lax.all_to_all(outgoing, name, 0, 0), axis=dim)]
  transfers between devices with their start and end apart: 4 -> 5, of which waited for: 3 -> 4; matrix products, arithmetic and copies ran while one was open for 1% -> 1% of each run, Pallas kernels for 0% -> 0%
where the time goes in v1:
time: 409 us; the launch traced here: 408 us
  waiting for transfers between devices  193 us (47%)
  matrix products  82.5 us (20%)
  local copies, waits for them, and re-layouts  56.6 us (14%)
  blocking collectives  38.1 us (9%)
  starting transfers between devices  21.4 us (5%)
  between operations  13.5 us (3%)
    reduce_scatter x1, waiting for transfers between devices, body(): lax.psum_scatter(partial_grad, 'mrow', scatter_dimension=0, tiled=True)  151 us
    dot_general x8, matrix products, head_terms(): jnp.einsum('kgte,ekd->tkgd', grad_scores, mem_keys, preferred_element_typ...  46.7 us
    all_gather x1, blocking collectives, body(): lax.all_gather(log_sum, 'mrow', axis=0, tiled=True)  38.1 us
    dot_general x8, matrix products, head_terms(): jnp.einsum('tkgd,ekd->kgte', query_heads, mem_keys, preferred_element_typ...  35.8 us
    all_gather x1, waiting for transfers between devices, body(): lax.all_gather(stacked, 'mrow', axis=0, tiled=True)  28.6 us
    dynamic_update_slice x8, local copies, waits for them, and re-layouts, block_terms(): terms = lax.map(one_block, (query_heads, grad_heads, log_heads, dot_heads))  13.4 us
    dynamic_slice x16, local copies, waits for them, and re-layouts, block_terms(): terms = lax.map(one_block, (query_heads, grad_heads, log_heads, dot_heads))  12.6 us
    all_to_all x1, starting transfers between devices, swapped_in(): return jnp.concatenate(lax.all_to_all(outgoing, name, 0, 0), axis=dim)  11.3 us
  transfers between devices with their start and end apart: 5, of which 4 were waited for; matrix products, arithmetic and copies ran while one was open for 1% of the time, Pallas kernels for 0%

profile of v1, /device:TPU:8, one launch (start us, length us, event | category | flops | bytes accessed | tf_op | source)
XLA Modules:
  0.0 408.2 jit_solution(15209784991498231551)
XLA Ops:
  10.3 11.3 %all-to-all-start.2 = ((f32[32,128,4]{1,2,0:T(4,128)}), f32[32,128,4]{1,2,0:T(4,128)S(1)}, u32[]{:S(2)}, u32[]{:S(2)}) async-start(f32[32,128,4]{1,2,0:T(4,128)} %stack.11), calls=%async_computation.2 | async-start | bytes 131072 | tf_op jit(solution)/shard_map/all_to_all | solution.py:13
  22.4 9.9 %all-to-all-done.2 = f32[32,128,4]{1,2,0:T(4,128)S(1)} async-done(((f32[32,128,4]{1,2,0:T(4,128)}), f32[32,128,4]{1,2,0:T(4,128)S(1)}, u32[]{:S(2)}, u32[]{:S(2)}) %all-to-all-start.2) | async-done | bytes 65568 | tf_op jit(solution)/shard_map/all_to_all | solution.py:13
  32.3 4.9 %all-to-all-start = ((bf16[8,16,8,128]{3,1,0,2:T(8,128)(2,1)}), bf16[8,16,8,128]{3,1,0,2:T(8,128)(2,1)S(1)}, u32[]{:S(2)}, u32[]{:S(2)}) async-start(bf16[8,16,8,128]{3,1,0,2:T(8,128)(2,1)} %copy_bitcast_fusion.8), calls=%async_computation | async-start | bytes 524288 | tf_op jit(solution)/shard_map/all_to_all | solution.py:74
  42.8 5.1 %all-to-all-start.1 = ((bf16[8,16,8,128]{3,1,0,2:T(8,128)(2,1)}), bf16[8,16,8,128]{3,1,0,2:T(8,128)(2,1)S(1)}, u32[]{:S(2)}, u32[]{:S(2)}) async-start(bf16[8,16,8,128]{3,1,0,2:T(8,128)(2,1)} %copy_bitcast_fusion.7), calls=%async_computation.1 | async-start | bytes 524288 | tf_op jit(solution)/shard_map/all_to_all | solution.py:75
  47.9 38.1 %all_gather.7 = f32[4096,4]{0,1:T(4,128)S(1)} all-gather(f32[128,4]{0,1:T(4,128)} %param.11), channel_id=1, replica_groups=mesh['mrow'=32,'mcol'=8] {'mrow'}, dimensions={0}, use_global_device_ids=true | all-gather | bytes 67584 | tf_op jit(solution)/shard_map/all_gather | solution.py:81
  86.1 28.6 %all-gather.2.cloned.1.call-done = bf16[4096,2,512]{2,0,1:T(8,128)(2,1)} async-done(((bf16[128,2,512]{2,0,1:T(8,128)(2,1)}), bf16[4096,2,512]{2,0,1:T(8,128)(2,1)}) %all-gather.2.cloned.1.call-update) | async-done | bytes 8388624 | tf_op jit(solution)/shard_map/all_gather | solution.py:87
  114.7 5.7 %fusion.20 = (bf16[4096,1,512]{2,0,1:T(8,128)(2,1)}, bf16[4096,1,512]{2,0,1:T(8,128)(2,1)}) fusion(bf16[4096,2,512]{2,0,1:T(8,128)(2,1)} %all-gather.2.cloned.1.call-done), kind=kLoop, calls=%fused_computation.28 | loop fusion | bytes 16777216 | tf_op jit(solution)/shard_map/slice | solution.py:49
  120.4 6.9 %reshape.67 = bf16[8,512,1,4,128]{4,3,1,0,2:T(4,128)(2,1)} reshape(bf16[4096,1,512]{2,0,1:T(8,128)(2,1)} %get-tuple-element.93) | data formatting | bytes 8388608 | tf_op jit(solution)/shard_map/reshape;squeeze | solution.py:48
  127.3 6.9 %reshape.68 = bf16[8,512,1,4,128]{4,3,1,0,2:T(4,128)(2,1)} reshape(bf16[4096,1,512]{2,0,1:T(8,128)(2,1)} %get-tuple-element.92) | data formatting | bytes 8388608 | tf_op jit(solution)/shard_map/reshape;squeeze | solution.py:49
  134.3 108.8 %while.10 = (s32[]{:T(128)}, f32[8,512,1,4,128]{4,3,1,0,2:T(4,128)}, bf16[8,512,1,4,128]{4,3,1,0,2:T(4,128)(2,1)}, bf16[1024,1,128]{2,0,1:T(8,128)(2,1)S(1)}, f3...) while((s32[]{:T(128)}, ...), condition=%wide.region_2.3_spmd, body=%wide.region_1.2_spmd.sunk | while | flops 1621360640 | bytes 23921256 | solution.py:57
  135.9 4.5 %fusion.33 = f32[512,4,1024]{2,0,1:T(8,128)} fusion(bf16[1,512,1,4,128]{4,3,1,0,2:T(4,128)(2,1)S(1)} %get-tuple-element.147, bf16[1024,1,128]{2,0,1:T(8,128)(2,1)S(1)} %get-tuple-element.172), kind=kOutput, calls=%fused_computation.13.clone.1 | convolution fusion | flops 536870912 | bytes 9175040 | tf_op jit(solution)/shard_map/while/body/eval_jaxpr/tkgd,ekd->kgte/dot_general | solution.py:27
  140.3 5.8 %fusion.34 = f32[1,512,1,4,128]{4,1,3,2,0:T(8,128)S(1)} fusion(f32[512,4,1024]{2,0,1:T(8,128)} %fusion.33, f32[4,512]{1,0:T(4,128)S(1)} %get-tuple-element.148, f32[4,512]{1,0:T(4,128)S(1)} %get-tuple-element.149, bf16[1,512,1,4,128]{4,3,1,0,2:T(4,128)(2,1)S(1)} %get-tuple-element.150, bf16[1024,1,128]{2,0,1:T(8,128)(2,1)S(1)} %get-tuple-element.175, ...), kind=kOutput, calls=%fused_computation.9.clone.1 | convolution fusion | flops 1084489728 | bytes 10502144 | tf_op jit(solution)/shard_map/while/body/eval_jaxpr/kgte,ekd->tkgd/dot_general | solution.py:35
  153.9 5.8 %fusion.34 = f32[1,512,1,4,128]{4,1,3,2,0:T(8,128)S(1)} fusion(f32[512,4,1024]{2,0,1:T(8,128)} %fusion.33, f32[4,512]{1,0:T(4,128)S(1)} %get-tuple-element.148, f32[4,512]{1,0:T(4,128)S(1)} %get-tuple-element.149, bf16[1,512,1,4,128]{4,3,1,0,2:T(4,128)(2,1)S(1)} %get-tuple-element.150, bf16[1024,1,128]{2,0,1:T(8,128)(2,1)S(1)} %get-tuple-element.175, ...), kind=kOutput, calls=%fused_computation.9.clone.1 | convolution fusion | flops 1084489728 | bytes 10502144 | tf_op jit(solution)/shard_map/while/body/eval_jaxpr/kgte,ekd->tkgd/dot_general | solution.py:35
  163.0 4.5 %fusion.33 = f32[512,4,1024]{2,0,1:T(8,128)} fusion(bf16[1,512,1,4,128]{4,3,1,0,2:T(4,128)(2,1)S(1)} %get-tuple-element.147, bf16[1024,1,128]{2,0,1:T(8,128)(2,1)S(1)} %get-tuple-element.172), kind=kOutput, calls=%fused_computation.13.clone.1 | convolution fusion | flops 536870912 | bytes 9175040 | tf_op jit(solution)/shard_map/while/body/eval_jaxpr/tkgd,ekd->kgte/dot_general | solution.py:27
  167.5 5.8 %fusion.34 = f32[1,512,1,4,128]{4,1,3,2,0:T(8,128)S(1)} fusion(f32[512,4,1024]{2,0,1:T(8,128)} %fusion.33, f32[4,512]{1,0:T(4,128)S(1)} %get-tuple-element.148, f32[4,512]{1,0:T(4,128)S(1)} %get-tuple-element.149, bf16[1,512,1,4,128]{4,3,1,0,2:T(4,128)(2,1)S(1)} %get-tuple-element.150, bf16[1024,1,128]{2,0,1:T(8,128)(2,1)S(1)} %get-tuple-element.175, ...), kind=kOutput, calls=%fused_computation.9.clone.1 | convolution fusion | flops 1084489728 | bytes 10502144 | tf_op jit(solution)/shard_map/while/body/eval_jaxpr/kgte,ekd->tkgd/dot_general | solution.py:35
  176.6 4.5 %fusion.33 = f32[512,4,1024]{2,0,1:T(8,128)} fusion(bf16[1,512,1,4,128]{4,3,1,0,2:T(4,128)(2,1)S(1)} %get-tuple-element.147, bf16[1024,1,128]{2,0,1:T(8,128)(2,1)S(1)} %get-tuple-element.172), kind=kOutput, calls=%fused_computation.13.clone.1 | convolution fusion | flops 536870912 | bytes 9175040 | tf_op jit(solution)/shard_map/while/body/eval_jaxpr/tkgd,ekd->kgte/dot_general | solution.py:27
  181.1 5.8 %fusion.34 = f32[1,512,1,4,128]{4,1,3,2,0:T(8,128)S(1)} fusion(f32[512,4,1024]{2,0,1:T(8,128)} %fusion.33, f32[4,512]{1,0:T(4,128)S(1)} %get-tuple-element.148, f32[4,512]{1,0:T(4,128)S(1)} %get-tuple-element.149, bf16[1,512,1,4,128]{4,3,1,0,2:T(4,128)(2,1)S(1)} %get-tuple-element.150, bf16[1024,1,128]{2,0,1:T(8,128)(2,1)S(1)} %get-tuple-element.175, ...), kind=kOutput, calls=%fused_computation.9.clone.1 | convolution fusion | flops 1084489728 | bytes 10502144 | tf_op jit(solution)/shard_map/while/body/eval_jaxpr/kgte,ekd->tkgd/dot_general | solution.py:35
  194.7 5.8 %fusion.34 = f32[1,512,1,4,128]{4,1,3,2,0:T(8,128)S(1)} fusion(f32[512,4,1024]{2,0,1:T(8,128)} %fusion.33, f32[4,512]{1,0:T(4,128)S(1)} %get-tuple-element.148, f32[4,512]{1,0:T(4,128)S(1)} %get-tuple-element.149, bf16[1,512,1,4,128]{4,3,1,0,2:T(4,128)(2,1)S(1)} %get-tuple-element.150, bf16[1024,1,128]{2,0,1:T(8,128)(2,1)S(1)} %get-tuple-element.175, ...), kind=kOutput, calls=%fused_computation.9.clone.1 | convolution fusion | flops 1084489728 | bytes 10502144 | tf_op jit(solution)/shard_map/while/body/eval_jaxpr/kgte,ekd->tkgd/dot_general | solution.py:35
  203.8 4.5 %fusion.33 = f32[512,4,1024]{2,0,1:T(8,128)} fusion(bf16[1,512,1,4,128]{4,3,1,0,2:T(4,128)(2,1)S(1)} %get-tuple-element.147, bf16[1024,1,128]{2,0,1:T(8,128)(2,1)S(1)} %get-tuple-element.172), kind=kOutput, calls=%fused_computation.13.clone.1 | convolution fusion | flops 536870912 | bytes 9175040 | tf_op jit(solution)/shard_map/while/body/eval_jaxpr/tkgd,ekd->kgte/dot_general | solution.py:27
  208.3 5.8 %fusion.34 = f32[1,512,1,4,128]{4,1,3,2,0:T(8,128)S(1)} fusion(f32[512,4,1024]{2,0,1:T(8,128)} %fusion.33, f32[4,512]{1,0:T(4,128)S(1)} %get-tuple-element.148, f32[4,512]{1,0:T(4,128)S(1)} %get-tuple-element.149, bf16[1,512,1,4,128]{4,3,1,0,2:T(4,128)(2,1)S(1)} %get-tuple-element.150, bf16[1024,1,128]{2,0,1:T(8,128)(2,1)S(1)} %get-tuple-element.175, ...), kind=kOutput, calls=%fused_computation.9.clone.1 | convolution fusion | flops 1084489728 | bytes 10502144 | tf_op jit(solution)/shard_map/while/body/eval_jaxpr/kgte,ekd->tkgd/dot_general | solution.py:35
  221.9 5.8 %fusion.34 = f32[1,512,1,4,128]{4,1,3,2,0:T(8,128)S(1)} fusion(f32[512,4,1024]{2,0,1:T(8,128)} %fusion.33, f32[4,512]{1,0:T(4,128)S(1)} %get-tuple-element.148, f32[4,512]{1,0:T(4,128)S(1)} %get-tuple-element.149, bf16[1,512,1,4,128]{4,3,1,0,2:T(4,128)(2,1)S(1)} %get-tuple-element.150, bf16[1024,1,128]{2,0,1:T(8,128)(2,1)S(1)} %get-tuple-element.175, ...), kind=kOutput, calls=%fused_computation.9.clone.1 | convolution fusion | flops 1084489728 | bytes 10502144 | tf_op jit(solution)/shard_map/while/body/eval_jaxpr/kgte,ekd->tkgd/dot_general | solution.py:35
  235.5 5.8 %fusion.34 = f32[1,512,1,4,128]{4,1,3,2,0:T(8,128)S(1)} fusion(f32[512,4,1024]{2,0,1:T(8,128)} %fusion.33, f32[4,512]{1,0:T(4,128)S(1)} %get-tuple-element.148, f32[4,512]{1,0:T(4,128)S(1)} %get-tuple-element.149, bf16[1,512,1,4,128]{4,3,1,0,2:T(4,128)(2,1)S(1)} %get-tuple-element.150, bf16[1024,1,128]{2,0,1:T(8,128)(2,1)S(1)} %get-tuple-element.175, ...), kind=kOutput, calls=%fused_computation.9.clone.1 | convolution fusion | flops 1084489728 | bytes 10502144 | tf_op jit(solution)/shard_map/while/body/eval_jaxpr/kgte,ekd->tkgd/dot_general | solution.py:35
  243.0 7.6 %copy.61 = f32[512,8,4,128]{3,1,2,0:T(8,128)} copy(f32[512,8,4,128]{3,2,1,0:T(4,128)} %bitcast.131) | data formatting | bytes 16777216
  250.6 150.7 %reduce-scatter.2.cloned.1.call-done = f32[128,512]{1,0:T(8,128)} async-done(((f32[4096,512]{1,0:T(8,128)}), f32[128,512]{1,0:T(8,128)}) %reduce-scatter.2.cloned.1.call-update) | async-done | bytes 262160 | tf_op jit(solution)/shard_map/reduce_scatter | solution.py:93
  (57 shorter events, 54.1 us)
Async XLA Ops:
  6.5 15.1 %copy-start = (bf16[8,16,1024]{2,1,0:T(8,128)(2,1)S(1)}, bf16[8,16,1024]{2,1,0:T(8,128)(2,1)}, u32[]{:S(2)}) copy-start(bf16[8,16,1024]{2,1,0:T(8,128)(2,1)} %param.12) | copy-start | bytes 786436
  6.5 108.2 %all-gather.2.cloned.1.call-start = ((), (), s32[]{:S(2)}) async-start(), calls=%async_computation.4 | async-start | bytes 8650752 | tf_op jit(solution)/shard_map/all_gather | solution.py:87
  10.3 22.0 %all-to-all-start.2 = ((f32[32,128,4]{1,2,0:T(4,128)}), f32[32,128,4]{1,2,0:T(4,128)S(1)}, u32[]{:S(2)}, u32[]{:S(2)}) async-start(f32[32,128,4]{1,2,0:T(4,128)} %stack.11), calls=%async_computation.2 | async-start | bytes 131072 | tf_op jit(solution)/shard_map/all_to_all | solution.py:13
  32.3 10.5 %all-to-all-start = ((bf16[8,16,8,128]{3,1,0,2:T(8,128)(2,1)}), bf16[8,16,8,128]{3,1,0,2:T(8,128)(2,1)S(1)}, u32[]{:S(2)}, u32[]{:S(2)}) async-start(bf16[8,16,8,128]{3,1,0,2:T(8,128)(2,1)} %copy_bitcast_fusion.8), calls=%async_computation | async-start | bytes 524288 | tf_op jit(solution)/shard_map/all_to_all | solution.py:74
  42.8 43.3 %all-to-all-start.1 = ((bf16[8,16,8,128]{3,1,0,2:T(8,128)(2,1)}), bf16[8,16,8,128]{3,1,0,2:T(8,128)(2,1)S(1)}, u32[]{:S(2)}, u32[]{:S(2)}) async-start(bf16[8,16,8,128]{3,1,0,2:T(8,128)(2,1)} %copy_bitcast_fusion.7), calls=%async_computation.1 | async-start | bytes 524288 | tf_op jit(solution)/shard_map/all_to_all | solution.py:75
  47.9 353.4 %reduce-scatter.2.cloned.1.call-start = ((), (), s32[]{:S(2)}) async-start(), calls=%async_computation.5 | async-start | bytes 8650752 | tf_op jit(solution)/shard_map/reduce_scatter | solution.py:93
Sparse Core Ops, SparseCore 0:
  10.2 104.4 all-gather.1
  250.8 150.5 reduce-scatter.1
